TPU v7x, 128 devices: a whole 4x4x4 slice. The times are simulated.
128 devices in a mesh: dp: 16 (over x_lo, z, core), mp: 8 (over x_hi, y).
Axes of the slice: x: 4 (x_hi: 2, x_lo: 2; x = x_hi * 2 + x_lo), y: 4, z: 4, core: 2. Of those that a mesh axis runs over, the one named last changes fastest.
Arguments:
- tokens: bfloat16 [16384, 2048], P('dp'), may hold values from -6 to 6
- lengths: int32 [16, 4], P('dp'), may hold values from 0 to 1024, as said below
- ln1_gain: float32 [2048], replicated, may hold values from 0.1 to 1.9
- ln1_bias: float32 [2048], replicated, may hold values from -4 to 4
- ln2_gain: float32 [2048], replicated, may hold values from 0.1 to 1.9
- ln2_bias: float32 [2048], replicated, may hold values from -4 to 4
- qkv_master: float32 [2048, 3, 2048], P(None, None, 'mp'), may hold values from -0.125 to 0.125
- qkv_bias: float32 [3, 2048], P(None, 'mp'), may hold values from -6 to 6
- out_master: float32 [2048, 2048], P('mp'), may hold values from -0.75 to 0.75
- up_master: float32 [2048, 8192], P(None, 'mp'), may hold values from -0.125 to 0.125
- up_bias: float32 [8192], P('mp'), may hold values from -6 to 6
- down_master: float32 [8192, 2048], P('mp'), may hold values from -0.0625 to 0.0625
- branch_bias: float32 [2048], replicated, may hold values from -4 to 4
- cotangent: bfloat16 [16384, 2048], P('dp'), may hold values from -6 to 6
Outputs:
- output: bfloat16 [16384, 2048], P('dp')
- grad_tokens: bfloat16 [16384, 2048], P('dp')
- grad_ln1_gain: float32 [2048], P('mp')
- grad_ln1_bias: float32 [2048], P('mp')
- grad_ln2_gain: float32 [2048], P('mp')
- grad_ln2_bias: float32 [2048], P('mp')
- grad_qkv: float32 [2048, 3, 2048], P('dp', None, 'mp')
- grad_qkv_bias: float32 [3, 2048], P(None, 'mp')
- grad_out: float32 [2048, 2048], P('mp', 'dp')
- grad_up: float32 [2048, 8192], P('dp', 'mp')
- grad_up_bias: float32 [8192], P('mp')
- grad_down: float32 [8192, 2048], P('mp', 'dp')
- grad_branch_bias: float32 [2048], P('mp')
Inputs may be any that keep to these rules, and one draw needn't show every extreme that they name: Row r of lengths describes bucket r: its sequences lie end to end from the bucket's first row in slot order and the rest of its 1024 rows are padding; a slot may be empty (length 0); each bucket's lengths sum to 512 or more; some bucket holds one sequence of exactly 1024.
All inputs are finite; a program needn't handle non-finite values.
Results may differ from a plain program's by a relative error of at most 0.012.
The roundings to bfloat16 on the way count: a program that leaves them out, or rounds other values in their place, can miss the bound.
Values may be sent and summed in bfloat16 or wider, within the bound.
A program may use at most 256 MiB of HBM per device.

v0:
```python
import math

import jax
import jax.numpy as jnp
from jax import lax
from jax.sharding import PartitionSpec as P

HS = 256
ROT = 64


norm_eps = 1e-05
masked_value = -1e30


def product_tn(first_mat, second_mat):
    return lax.dot_general(
        first_mat, second_mat, (((0,), (0,)), ((), ())), preferred_element_type=jnp.float32
    )


def product_nt(first_mat, second_mat):
    return lax.dot_general(
        first_mat, second_mat, (((1,), (1,)), ((), ())), preferred_element_type=jnp.float32
    )


def layout(seq_lengths, row_count):
    seq_ends = jnp.cumsum(seq_lengths)
    seq_starts = seq_ends - seq_lengths
    token_index = jnp.arange(row_count, dtype=jnp.int32)
    segment = jnp.sum((token_index[:, None] >= seq_ends[None, :]).astype(jnp.int32), axis=1)
    slot_ids = jnp.arange(seq_lengths.shape[0], dtype=jnp.int32)
    seq_first = jnp.sum(
        jnp.where(segment[:, None] == slot_ids[None, :], seq_starts[None, :], 0), axis=1
    )
    return (segment, token_index - seq_first)


def angles(position):
    inv_freq = jnp.exp(jnp.arange(ROT // 2, dtype=jnp.float32) * (-2.0 * math.log(10000.0) / ROT))
    phases = position.astype(jnp.float32)[:, None] * inv_freq[None, :]
    return (jnp.cos(phases)[:, None, :], jnp.sin(phases)[:, None, :])


def rotate(heads_in, cos_of, sin_of):
    half_rot = ROT // 2
    low_half = heads_in[..., :half_rot]
    high_half = heads_in[..., half_rot:ROT]
    return jnp.concatenate(
        [
            low_half * cos_of - high_half * sin_of,
            high_half * cos_of + low_half * sin_of,
            heads_in[..., ROT:],
        ],
        axis=-1,
    )


def unrotate(grad_in, cos_of, sin_of):
    half_rot = ROT // 2
    low_half = grad_in[..., :half_rot]
    high_half = grad_in[..., half_rot:ROT]
    return jnp.concatenate(
        [
            low_half * cos_of + high_half * sin_of,
            high_half * cos_of - low_half * sin_of,
            grad_in[..., ROT:],
        ],
        axis=-1,
    )


def gelu_exact(values_in):
    return jax.nn.gelu(values_in, approximate=False)


def masked_scores(query_block, keys, allowed, scale):
    scores = (
        jnp.einsum("qhd,khd->hqk", query_block, keys, preferred_element_type=jnp.float32) * scale
    )
    return jnp.where(allowed[None], scores, masked_value)


def norm_back(grad_norm, gain, normed, inv_std):
    scaled = grad_norm * gain
    return inv_std * (
        scaled
        - jnp.mean(scaled, axis=-1, keepdims=True)
        - normed * jnp.mean(scaled * normed, axis=-1, keepdims=True)
    )


def local(
    tokens,
    lengths,
    ln1_gain,
    ln1_bias,
    ln2_gain,
    ln2_bias,
    qkv_master,
    qkv_bias,
    out_master,
    up_master,
    up_bias,
    down_master,
    branch_bias,
    cotangent,
):
    row_count, model_width = tokens.shape
    mp_size = lax.axis_size("mp")
    mp_rank = lax.axis_index("mp")
    col_share = model_width // mp_size
    local_cols = qkv_master.shape[2]
    local_heads = local_cols // HS
    scale = 1.0 / math.sqrt(HS)
    slot_count = lengths.shape[1]
    segment, position = layout(lengths[0], row_count)
    valid_rows = (segment < slot_count).astype(jnp.float32)[:, None]
    token_index = jnp.arange(row_count, dtype=jnp.int32)
    inputs = tokens.astype(jnp.float32)
    row_mean = jnp.mean(inputs, axis=-1, keepdims=True)
    centred = inputs - row_mean
    row_var = jnp.mean(centred * centred, axis=-1, keepdims=True)
    inv_std = lax.rsqrt(row_var + norm_eps)
    normed = centred * inv_std
    attn_in = (normed * ln1_gain + ln1_bias).astype(jnp.bfloat16)
    mlp_in = (normed * ln2_gain + ln2_bias).astype(jnp.bfloat16)
    w_qkv = qkv_master.astype(jnp.bfloat16).reshape(model_width, 3 * local_cols)
    w_out = out_master.astype(jnp.bfloat16)
    w_up = up_master.astype(jnp.bfloat16)
    w_down = down_master.astype(jnp.bfloat16)
    projected = jnp.dot(attn_in, w_qkv, preferred_element_type=jnp.float32) + qkv_bias.reshape(
        3 * local_cols
    )
    projected = projected.reshape(row_count, 3, local_heads, HS)
    cos_of, sin_of = angles(position)
    query = rotate(projected[:, 0], cos_of, sin_of).astype(jnp.bfloat16)
    keys = rotate(projected[:, 1], cos_of, sin_of).astype(jnp.bfloat16)
    values = projected[:, 2].astype(jnp.bfloat16)
    row_block = min(512, row_count)
    block_starts = list(range(0, row_count, row_block))
    head_outs = []
    log_sums = []
    for first_row in block_starts:
        allowed = (segment[first_row : first_row + row_block, None] == segment[None, :]) & (
            token_index[first_row : first_row + row_block, None] >= token_index[None, :]
        )
        scores = masked_scores(query[first_row : first_row + row_block], keys, allowed, scale)
        row_max = jnp.max(scores, axis=-1, keepdims=True)
        weights = jnp.exp(scores - row_max)
        row_total = jnp.sum(weights, axis=-1, keepdims=True)
        probs_low = (weights / row_total).astype(jnp.bfloat16)
        log_sums.append(row_max + jnp.log(row_total))
        head_outs.append(
            jnp.einsum("hqk,khd->qhd", probs_low, values, preferred_element_type=jnp.float32)
        )
    mixed = jnp.concatenate(head_outs, axis=0).reshape(row_count, local_cols).astype(jnp.bfloat16)
    up_pre = jnp.dot(mlp_in, w_up, preferred_element_type=jnp.float32) + up_bias
    activation, gelu_back = jax.vjp(gelu_exact, up_pre)
    activation_low = activation.astype(jnp.bfloat16)
    branch_part = jnp.dot(mixed, w_out, preferred_element_type=jnp.float32) + jnp.dot(
        activation_low, w_down, preferred_element_type=jnp.float32
    )
    branch_total = lax.psum(branch_part, "mp")
    output = (valid_rows * (inputs + branch_total + branch_bias)).astype(jnp.bfloat16)
    grad_rows = valid_rows * cotangent.astype(jnp.float32)
    grad_low = grad_rows.astype(jnp.bfloat16)
    bias_total = jnp.sum(grad_rows, axis=0)
    grad_act = product_nt(grad_low, w_down)
    (grad_up_pre,) = gelu_back(grad_act)
    grad_up_low = grad_up_pre.astype(jnp.bfloat16)
    down_weight_grad = product_tn(activation_low, grad_low)
    up_weight_grad = product_tn(mlp_in, grad_up_low)
    up_bias_grad = jnp.sum(grad_up_low, axis=0, dtype=jnp.float32)
    mlp_grad_in = product_nt(grad_up_low, w_up)
    grad_mixed = (
        product_nt(grad_low, w_out).astype(jnp.bfloat16).reshape(row_count, local_heads, HS)
    )
    out_weight_grad = product_tn(mixed, grad_low)
    query_grads = []
    key_grad = jnp.zeros((row_count, local_heads, HS), jnp.float32)
    value_grad = jnp.zeros((row_count, local_heads, HS), jnp.float32)
    for block_number, first_row in enumerate(block_starts):
        allowed = (segment[first_row : first_row + row_block, None] == segment[None, :]) & (
            token_index[first_row : first_row + row_block, None] >= token_index[None, :]
        )
        query_rows = query[first_row : first_row + row_block]
        mixed_grad_rows = grad_mixed[first_row : first_row + row_block]
        scores = masked_scores(query_rows, keys, allowed, scale)
        probs = jnp.exp(scores - log_sums[block_number])
        prob_grad = jnp.einsum(
            "qhd,khd->hqk", mixed_grad_rows, values, preferred_element_type=jnp.float32
        )
        prob_dot = jnp.sum(probs * prob_grad, axis=-1, keepdims=True)
        score_grad = (probs * (prob_grad - prob_dot)).astype(jnp.bfloat16)
        query_grads.append(
            jnp.einsum("hqk,khd->qhd", score_grad, keys, preferred_element_type=jnp.float32) * scale
        )
        key_grad = (
            key_grad
            + jnp.einsum("hqk,qhd->khd", score_grad, query_rows, preferred_element_type=jnp.float32)
            * scale
        )
        value_grad = value_grad + jnp.einsum(
            "hqk,qhd->khd",
            probs.astype(jnp.bfloat16),
            mixed_grad_rows,
            preferred_element_type=jnp.float32,
        )
    query_grad = jnp.concatenate(query_grads, axis=0)
    qkv_grad_low = (
        jnp.stack(
            [unrotate(query_grad, cos_of, sin_of), unrotate(key_grad, cos_of, sin_of), value_grad],
            axis=1,
        )
        .astype(jnp.bfloat16)
        .reshape(row_count, 3 * local_cols)
    )
    qkv_weight_grad = product_tn(attn_in, qkv_grad_low).reshape(model_width, 3, local_cols)
    qkv_bias_grad = jnp.sum(qkv_grad_low, axis=0, dtype=jnp.float32).reshape(3, local_cols)
    attn_grad_in = product_nt(qkv_grad_low, w_qkv)
    partial_input = norm_back(attn_grad_in, ln1_gain, normed, inv_std) + norm_back(
        mlp_grad_in, ln2_gain, normed, inv_std
    )
    gain_part = jnp.stack(
        [
            jnp.sum(attn_grad_in * normed, axis=0),
            jnp.sum(attn_grad_in, axis=0),
            jnp.sum(mlp_grad_in * normed, axis=0),
            jnp.sum(mlp_grad_in, axis=0),
        ]
    )
    input_total, gain_total = lax.psum((partial_input, gain_part), "mp")
    grad_tokens = (input_total + grad_rows).astype(jnp.bfloat16)
    gain_share = lax.dynamic_slice_in_dim(gain_total, mp_rank * col_share, col_share, 1)
    bias_share = lax.dynamic_slice_in_dim(bias_total, mp_rank * col_share, col_share, 0)
    qkv_bias_sum, up_bias_sum, gain_sums, bias_sum = lax.psum(
        (qkv_bias_grad, up_bias_grad, gain_share, bias_share), "dp"
    )
    qkv_grad_share, out_grad_share, up_grad_share, down_grad_share = (
        lax.psum_scatter(qkv_weight_grad, "dp", scatter_dimension=0, tiled=True),
        lax.psum_scatter(out_weight_grad, "dp", scatter_dimension=1, tiled=True),
        lax.psum_scatter(up_weight_grad, "dp", scatter_dimension=0, tiled=True),
        lax.psum_scatter(down_weight_grad, "dp", scatter_dimension=1, tiled=True),
    )
    return (
        output,
        grad_tokens,
        gain_sums[0],
        gain_sums[1],
        gain_sums[2],
        gain_sums[3],
        qkv_grad_share,
        qkv_bias_sum,
        out_grad_share,
        up_grad_share,
        up_bias_sum,
        down_grad_share,
        bias_sum,
    )


def solution(mesh):
    placed = (
        P("dp", None),
        P("dp", None),
        P(),
        P(),
        P(),
        P(),
        P(None, None, "mp"),
        P(None, "mp"),
        P("mp", None),
        P(None, "mp"),
        P("mp"),
        P("mp", None),
        P(),
        P("dp", None),
    )
    return jax.shard_map(
        local,
        mesh=mesh,
        in_specs=placed,
        out_specs=(
            P("dp", None),
            P("dp", None),
            P("mp"),
            P("mp"),
            P("mp"),
            P("mp"),
            P("dp", None, "mp"),
            P(None, "mp"),
            P("mp", "dp"),
            P("dp", "mp"),
            P("mp"),
            P("mp", "dp"),
            P("mp"),
        ),
        check_vma=False,
    )
```

profile of v0, /device:TPU:0, one launch (start us, length us, event | category | flops | bytes accessed | tf_op | source)
XLA Modules:
  0.0 660.0 jit_solution(12436382178309702079)
XLA Ops:
  8.1 0.8 reduce-window.4
  9.8 0.7 add.142
  10.5 3.0 convert_reduce_fusion
  13.9 1.2 fusion.22
  15.2 4.1 copy.34
  19.3 6.3 convolution_add_fusion.1
  26.6 0.8 fusion.125
  28.6 0.8 fusion.126
  29.8 1.3 fusion.58
  31.2 0.9 copy-done.2
  32.8 1.3 convolution_convert_fusion
  39.5 1.0 slice-done.2
  40.5 1.1 copy-done.1
  41.6 16.2 %multiply_convert_fusion = (bf16[1024,1024]{1,0:T(8,128)(2,1)}, f32[1024,1024]{1,0:T(8,128)}, f32[1024,1024]{1,0:T(8,128)}) fusion(f32[1024]{0:T(1024)S(1)} %copy-done.14, f32[2048,1024]{1,0:T(8,128)S(1)} %bitcast.122, bf16[1024,2048]{1,0:T(8,128)(2,1)S(1)} %copy-done.1, f32[2048]{0:T(1024)S(1)} %copy-done.13, f32[2048]{0:T(1024)S(1)} %copy-done.10, ...), kind=kOutput, calls=%fused_computation.42 | convolution fusion | flops 4378853376 | bytes 23097344 | tf_op jit(solution)/shard_map/dot_general | solution.py:159
  57.7 12.0 %convert_reduce_fusion.1 = (f32[1024]{0:T(1024)S(1)}, bf16[1024,1024]{1,0:T(8,128)(2,1)}) fusion(f32[1024,1024]{1,0:T(8,128)} %get-tuple-element.37, f32[1024,2048]{1,0:T(8,128)} %param.25, bf16[1024,2048]{1,0:T(8,128)(2,1)S(1)} %copy-done.2, f32[1024]{0:T(1024)S(1)} %compare_convert_fusion, f32[1024,1024]{1,0:T(8,128)} %get-tuple-element.58, ...), kind=kOutput, calls=%fused_computation.40 | convolution fusion | flops 4321180672 | bytes 23080960 | tf_op jit(solution)/shard_map/dot_general | solution.py:23
  69.7 7.8 %fusion.42 = f32[1024,2048]{1,0:T(8,128)S(1)} fusion(bf16[1024,1024]{1,0:T(8,128)(2,1)} %get-tuple-element.69, f32[2048,1024]{1,0:T(8,128)} %param.23), kind=kOutput, calls=%fused_computation.68 | convolution fusion | flops 4297064448 | bytes 18874368 | tf_op jit(solution)/shard_map/dot_general | solution.py:23
  79.2 8.5 %fusion.20 = (f32[2048]{0:T(1024)S(1)}, f32[1024]{0:T(1024)S(1)}, f32[1024]{0:T(1024)S(1)}, f32[2048]{0:T(1024)S(1)}, f32[2048]{0:T(1024)S(1)}, /*index=5*/f32[1...) fusion(bf16[1024,2048]{1,0:T(8,128)(2,1)S(1)} %copy-done.1, f32[1024]{0:T(1024)S(1)} %add_rsqrt_fusion, ...), kind=kOutput, calls=%fused_computation.23 | convolution fusion | flops 3256864768 | bytes 25763840 | tf_op jit(solution)/shard_map/dot_general | solution.py:23
  87.7 12.3 %fusion.38 = f32[1024,2048]{1,0:T(8,128)} fusion(bf16[1024,1024]{1,0:T(8,128)(2,1)} %get-tuple-element.36, f32[1024,2048]{1,0:T(8,128)} %param.25), kind=kOutput, calls=%fused_computation.66 | convolution fusion | flops 4297064448 | bytes 18874368 | tf_op jit(solution)/shard_map/dot_general | solution.py:162
  100.0 7.9 %convolution_add_fusion = f32[1024,2048]{1,0:T(8,128)} fusion(f32[1024,2048]{1,0:T(8,128)} %fusion.38, f32[256,2048]{1,0:T(8,128)S(1)} %copy-done.4, bf16[512,1,256]{0,2,1:T(8,128)(2,1)S(1)} %fusion.59, bf16[512,1,256]{0,2,1:T(8,128)(2,1)S(1)} %copy-done.7), kind=kOutput, calls=%fused_computation.36 | convolution fusion | flops 1077411840 | bytes 19398656 | tf_op jit(solution)/shard_map/dot_general | solution.py:162
  107.9 5.8 fusion.17
  113.8 5.0 fusion.71
  118.8 9.3 %fusion.29 = f32[2048,3,256]{2,0,1:T(8,128)} fusion(bf16[1024,3,1,256]{0,3,2,1:T(8,128)(2,1)S(1)} %copy-done.6, bf16[1024,2048]{1,0:T(8,128)(2,1)} %param.14, f32[2048]{0:T(1024)S(1)} %copy-done.12, f32[2048]{0:T(1024)S(1)} %copy-done.9, f32[1024]{0:T(1024)S(1)} %add_rsqrt_fusion, f32[1024]{0:T(1024)S(1)} %broadcast_multiply_fusion.4), kind=kOutput, calls=%fused_computation.38 | convolution fusion | flops 3233808384 | bytes 12083200 | tf_op jit(solution)/shard_map/dot_general | solution.py:17
  128.2 1.5 copy-done.16
  129.7 10.1 %fusion.114 = f32[2048,1024]{1,0:T(8,128)} fusion(bf16[1024,1024]{1,0:T(8,128)(2,1)S(1)} %copy-done.16, bf16[1024,2048]{1,0:T(8,128)(2,1)} %param.14, f32[2048]{0:T(1024)S(1)} %copy-done.13, f32[2048]{0:T(1024)S(1)} %copy-done.10, f32[1024]{0:T(1024)S(1)} %add_rsqrt_fusion, f32[1024]{0:T(1024)S(1)} %broadcast_multiply_fusion.4), kind=kOutput, calls=%fused_computation.187 | convolution fusion | flops 4307550208 | bytes 14704640 | tf_op jit(solution)/shard_map/dot_general | solution.py:17
  139.9 1.6 copy-done.15
  141.5 9.4 %fusion.117 = f32[1024,2048]{1,0:T(8,128)} fusion(bf16[1024,1024]{1,0:T(8,128)(2,1)S(1)} %copy-done.15, bf16[1024,2048]{1,0:T(8,128)(2,1)} %param.27, f32[1024]{0:T(1024)S(1)} %compare_convert_fusion), kind=kOutput, calls=%fused_computation.188 | convolution fusion | flops 4301258752 | bytes 14684160 | tf_op jit(solution)/shard_map/dot_general | solution.py:17
  151.0 44.0 %psum.51 = f32[4,2048]{1,0:T(4,128)S(1)} all-reduce(f32[4,2048]{1,0:T(4,128)S(1)} %pad_maximum_fusion.4), channel_id=1, replica_groups=mesh['dp'=16,'mp'=8] {'mp'}, use_global_device_ids=true, to_apply=%region_21.22 | all-reduce | flops 8192 | bytes 65536 | tf_op jit(solution)/shard_map/psum | solution.py:234
  195.0 304.6 %all-reduce.4.cloned.1.call-done = (f32[1024,2048]{1,0:T(8,128)}, f32[1024,2048]{1,0:T(8,128)}) async-done(((f32[1024,2048]{1,0:T(8,128)}, f32[1024,2048]{1,0:T(8,128)}), (f32[1024,2048]{1,0:T(8,128)}, f32[1024,2048]{1,0:T(8,128)})) %all-reduce.4.cloned.1.call-update) | async-done | bytes 16777232 | tf_op jit(solution)/shard_map/psum | solution.py:165
  499.5 13.5 %fusion.26 = (f32[2048]{0:T(1024)S(1)}, bf16[1024,2048]{1,0:T(8,128)(2,1)}, bf16[1024,2048]{1,0:T(8,128)(2,1)}) fusion(bf16[1024,2048]{1,0:T(8,128)(2,1)} %param.27, f32[1024]{0:T(1024)S(1)} %compare_convert_fusion, f32[1024,2048]{1,0:T(8,128)} %get-tuple-element.30, f32[2048]{0:T(1024)S(1)} %copy-done.11, f32[1024,2048]{1,0:T(8,128)} %get-tuple-element.29, ...), kind=kLoop, calls=%fused_computation.31 | loop fusion | flops 20969472 | bytes 33574912 | tf_op jit(solution)/shard_map/reduce_sum | solution.py:169
  513.1 55.3 %all-reduce = (f32[4,256]{1,0:T(4,128)S(1)}, f32[3,256]{1,0:T(4,128)}, f32[1024]{0:T(1024)}, f32[256]{0:T(256)}) all-reduce(f32[4,256]{1,0:T(4,128)S(1)} %constant_dynamic-slice_fusion, f32[3,256]{1,0:T(4,128)S(1)} %get-tuple-element.31, f32[1024]{0:T(1024)S(1)} %get-tuple-element.68, ...), channel_id=1, replica_groups=mesh['dp'=16,'mp'=8] {'dp'}, use_global_device_ids=true, to_apply=%region_22.23 | all-reduce | flops 3072 | bytes 24576 | tf_op jit(solution)/shard_map/psum | solution.py:238
  569.0 7.1 %reduce-scatter.9.cloned.1.call-done = f32[128,1024]{1,0:T(8,128)} async-done(((f32[2048,1024]{1,0:T(8,128)}), f32[128,1024]{1,0:T(8,128)}) %reduce-scatter.9.cloned.1.call-update) | async-done | bytes 524304 | tf_op jit(solution)/shard_map/reduce_scatter | solution.py:244
  576.1 76.1 %reduce-scatter.11.cloned.1.call-done = f32[1024,128]{1,0:T(8,128)} async-done(((f32[1024,2048]{1,0:T(8,128)}), f32[1024,128]{1,0:T(8,128)}) %reduce-scatter.11.cloned.1.call-update) | async-done | bytes 524304 | tf_op jit(solution)/shard_map/reduce_scatter | solution.py:245
  (93 shorter events, 12.5 us)
Async XLA Ops:
  8.0 491.5 %all-reduce.4.cloned.1.call-start = ((), (), s32[]{:S(2)}) async-start(), calls=%async_computation.8 | async-start | bytes 33554432 | tf_op jit(solution)/shard_map/psum | solution.py:165
  10.5 3.4 copy-start
  15.2 4.1 copy-start.8
  15.2 4.1 copy-start.9
  15.2 4.1 copy-start.12
  27.9 0.7 slice-start
  29.8 2.3 copy-start.2
  29.8 3.0 copy-start.3
  36.8 2.7 slice-start.1
  38.0 2.5 slice-start.2
  38.4 3.1 copy-start.1
  38.5 3.1 copy-start.10
  38.5 3.1 copy-start.13
  38.5 3.1 copy-start.14
  79.2 8.5 %copy-start.5 = (bf16[1024,3,1,256]{0,3,2,1:T(8,128)(2,1)}, bf16[1024,3,1,256]{0,3,2,1:T(8,128)(2,1)S(1)}, u32[]{:S(2)}) copy-start(bf16[1024,3,1,256]{0,3,2,1:T(8,128)(2,1)S(1)} %get-tuple-element.32) | copy-start | bytes 4718596
  87.7 12.3 %copy-start.4 = (f32[256,2048]{1,0:T(8,128)S(1)}, f32[256,2048]{1,0:T(8,128)}, u32[]{:S(2)}) copy-start(f32[256,2048]{1,0:T(8,128)} %param.22) | copy-start | bytes 6291460
  87.7 12.3 %copy-start.7 = (bf16[512,1,256]{0,2,1:T(8,128)(2,1)S(1)}, bf16[512,1,256]{0,2,1:T(8,128)(2,1)}, u32[]{:S(2)}) copy-start(bf16[512,1,256]{0,2,1:T(8,128)(2,1)} %fusion.58) | copy-start | bytes 786436
  113.7 5.1 copy-start.6
  113.7 455.2 %reduce-scatter.7.cloned.1.call-start = ((), (), s32[]{:S(2)}) async-start(), calls=%async_computation.5 | async-start | bytes 2228224 | tf_op jit(solution)/shard_map/reduce_scatter | solution.py:243
  118.8 450.2 %reduce-scatter.5.cloned.1.call-start = ((), (), s32[]{:S(2)}) async-start(), calls=%async_computation.4 | async-start | bytes 6684672 | tf_op jit(solution)/shard_map/reduce_scatter | solution.py:242
  128.1 1.6 copy-start.16
  128.1 448.0 %reduce-scatter.9.cloned.1.call-start = ((), (), s32[]{:S(2)}) async-start(), calls=%async_computation.6 | async-start | bytes 8912896 | tf_op jit(solution)/shard_map/reduce_scatter | solution.py:244
  139.8 1.7 copy-start.15
  139.9 512.4 %reduce-scatter.11.cloned.1.call-start = ((), (), s32[]{:S(2)}) async-start(), calls=%async_computation.7 | async-start | bytes 8912896 | tf_op jit(solution)/shard_map/reduce_scatter | solution.py:245
  150.9 348.7 %copy-start.11 = (f32[2048]{0:T(1024)S(1)}, f32[2048]{0:T(1024)}, u32[]{:S(2)}) copy-start(f32[2048]{0:T(1024)} %param.26) | copy-start | bytes 24580
Sparse Core Ops, SparseCore 0:
  113.9 385.6 all-reduce.3
Sparse Core Ops, SparseCore 1:
  118.9 171.2 reduce-scatter.6
  293.0 201.6 reduce-scatter.4
  497.5 78.6 reduce-scatter.8
  579.1 73.1 reduce-scatter.10
where the time goes:
time: 664 us; the launch traced here: 660 us
  waiting for transfers between devices  388 us (58%)
  matrix products  114 us (17%)
  blocking collectives  99.3 us (15%)
  other arithmetic  29.4 us (4%)
  between operations  16.4 us (2%)
  local copies, waits for them, and re-layouts  13.1 us (2%)
    psum x1, waiting for transfers between devices, local(): branch_total = lax.psum(branch_part, 'mp')  305 us
    reduce_scatter x1, waiting for transfers between devices, local(): lax.psum_scatter(down_weight_grad, 'dp', scatter_dimension=1, tiled=True)  76.1 us
    psum x1, blocking collectives, local(): lax.psum((qkv_bias_grad, up_bias_grad, gain_share, bias_share), 'dp')  55.3 us
    psum x1, blocking collectives, local(): input_total, gain_total = lax.psum((partial_input, gain_part), 'mp')  44 us
    dot_general x4, matrix products, product_tn(): lax.dot_general(first_mat, second_mat, (((0,), (0,)), ((), ())), preferre...  33.8 us
    dot_general x4, matrix products, product_nt(): lax.dot_general(first_mat, second_mat, (((1,), (1,)), ((), ())), preferre...  29.7 us
    dot_general x1, matrix products, local(): up_pre = jnp.dot(mlp_in, w_up, preferred_element_type=jnp.float32) + up_bias  16.2 us
    reduce_sum x1, other arithmetic, local(): bias_total = jnp.sum(grad_rows, axis=0)  13.5 us
  transfers between devices with their start and end apart: 5, of which 3 were waited for; matrix products, arithmetic and copies ran while one was open for 7% of the time, Pallas kernels for 0%

commit v1 on v0

v1 whole, which is shorter than its diff:
```python
import functools
import math

import jax
import jax.numpy as jnp
import numpy as np
from jax import lax
from jax.experimental import pallas as pl
from jax.experimental.pallas import tpu as pltpu
from jax.sharding import PartitionSpec as P

HS = 256
ROT = 64
BLK = 256
HALF = 128
SUB = 64
LEFT_COLS = 1152
MESH = pl.DeviceIdType.MESH
MIB = 2**20
norm_eps = 1e-05
masked_value = -1e30
f32 = jnp.float32
bf16 = jnp.bfloat16


def dot_nn(a, b):
    return jnp.dot(a, b, preferred_element_type=f32)


def dot_nt(a, b):
    return lax.dot_general(a, b, (((1,), (1,)), ((), ())), preferred_element_type=f32)


def dot_tn(a, b):
    return lax.dot_general(a, b, (((0,), (0,)), ((), ())), preferred_element_type=f32)


def aligned(start, size, unit=None):
    if isinstance(start, int):
        return pl.ds(start, size)
    return pl.ds(pl.multiple_of(start, unit or size), size)


class Place:
    def __init__(self):
        self.dp = lax.axis_index("dp")
        self.mp = lax.axis_index("mp")
        self.x_hi = self.mp // 4
        self.y = self.mp % 4
        self.x_lo = self.dp // 8
        self.z = (self.dp // 2) % 4
        self.core = self.dp % 2

    def y_at(self, off):
        return (self.y + off) % 4

    def z_at(self, off):
        return (self.z + off) % 4

    def to_y(self, y):
        return (self.dp, self.x_hi * 4 + y)

    def ring_y(self):
        right, left = self.y_at(1), self.y_at(3)
        return self.y, right, self.y_at(2), left, self.to_y(right), self.to_y(left)

    def ring_z(self):
        right, left = self.z_at(1), self.z_at(3)
        return self.z, right, self.z_at(2), left, self.to_z(right), self.to_z(left)

    def to_x_hi(self):
        return (self.dp, (1 - self.x_hi) * 4 + self.y)

    def to_z(self, z):
        return ((self.x_lo * 4 + z) * 2 + self.core, self.mp)

    def to_x_lo(self):
        return (((1 - self.x_lo) * 4 + self.z) * 2 + self.core, self.mp)

    def to_core(self):
        return ((self.x_lo * 4 + self.z) * 2 + 1 - self.core, self.mp)


def greet(targets):
    barrier = pltpu.get_barrier_semaphore()
    for target in targets:
        pl.semaphore_signal(barrier, inc=1, device_id=target, device_id_type=MESH)
    pl.semaphore_wait(barrier, len(targets))


class Link:
    def __init__(self, sems, number, src, dst, target):
        self.copy = pltpu.make_async_remote_copy(
            src_ref=src,
            dst_ref=dst,
            send_sem=sems.at[0, number],
            recv_sem=sems.at[1, number],
            device_id=target,
            device_id_type=MESH,
        )

    def start(self):
        self.copy.start()

    def got(self):
        self.copy.wait_recv()

    def sent(self):
        self.copy.wait_send()


class RingSum:
    def __init__(self, ring, src, rows, cols, buf, sems, base):
        self.src, self.rows, self.cols, self.buf = src, rows, cols, buf
        self.own, self.right, self.opp, self.left, to_right, to_left = ring
        part = self.part
        self.links = [
            Link(sems, base + 0, part(self.opp, 0), buf.at[0], to_right),
            Link(sems, base + 1, part(self.opp, 1), buf.at[1], to_left),
            Link(sems, base + 2, part(self.right, 0), buf.at[2], to_right),
            Link(sems, base + 3, part(self.right, 1), buf.at[3], to_right),
            Link(sems, base + 4, part(self.left, 1), buf.at[4], to_left),
            Link(sems, base + 5, part(self.left, 0), buf.at[5], to_left),
        ]

    def part(self, place, half):
        return self.src.at[self.rows(place, half), self.cols]

    def send_opp(self):
        self.links[0].start()
        self.links[1].start()

    def send_right(self):
        self.links[3].start()

    def send_left(self):
        self.links[5].start()

    def relay(self):
        for number, place, half in ((0, self.right, 0), (1, self.left, 1)):
            self.links[number].got()
            rows = self.rows(place, half)
            self.src[rows, self.cols] = (
                self.src[rows, self.cols].astype(f32) + self.buf[number].astype(f32)
            ).astype(bf16)
            self.links[2 if number == 0 else 4].start()

    def total(self, half):
        one, two = (2, 5) if half == 0 else (4, 3)
        self.links[one].got()
        self.links[two].got()
        own = self.src[self.rows(self.own, half), self.cols].astype(f32)
        return own + self.buf[one].astype(f32) + self.buf[two].astype(f32)

    def finish(self):
        for link in self.links:
            link.sent()


class BucketSum:
    LINKS = 17

    def __init__(self, here, src, buf_wide, buf_cut, buf_x, buf_far, stage, sems, width):
        self.here, self.src, self.buf_x, self.buf_far, self.stage = here, src, buf_x, buf_far, stage
        self.wide = pl.ds(0, width)
        self.cut, self.rest = pl.ds(0, LEFT_COLS), pl.ds(LEFT_COLS, width - LEFT_COLS)
        self.first_own = lambda y: y * BLK + here.x_hi * HALF
        self.first_far = lambda y: y * BLK + (1 - here.x_hi) * HALF
        halves = lambda first: lambda y, half: aligned(first(y) + half * SUB, SUB)
        self.far = RingSum(here.ring_y(), src, halves(self.first_far), self.cut, buf_cut, sems, 0)
        self.near = RingSum(here.ring_y(), src, halves(self.first_own), self.wide, buf_wide, sems, 6)
        self.across = [
            Link(
                sems,
                12 + off,
                src.at[aligned(self.first_far(here.y_at(off)), HALF), self.rest],
                buf_x.at[off],
                here.to_x_hi(),
            )
            for off in range(4)
        ]
        self.last = Link(sems, 16, stage, buf_far, here.to_x_hi())

    def add_across(self, off):
        self.across[off].got()
        rows = aligned(self.first_own(self.here.y_at(off)), HALF)
        self.src[rows, self.rest] = (
            self.src[rows, self.rest].astype(f32) + self.buf_x[off].astype(f32)
        ).astype(bf16)

    def pass_far(self):
        for half in range(2):
            self.stage[pl.ds(half * SUB, SUB), :] = self.far.total(half).astype(bf16)
        self.last.start()

    def finish(self):
        self.far.finish()
        self.near.finish()
        for link in self.across:
            link.sent()
        self.last.sent()


def gelu_parts(v):
    cdf = 0.5 * (1.0 + lax.erf(v * (1.0 / math.sqrt(2.0))))
    slope = cdf + v * (jnp.exp(-0.5 * v * v) * (1.0 / math.sqrt(2.0 * math.pi)))
    return v * cdf, slope


def row_stats(load, width):
    tiles = width // 128
    total = load(0)
    for tile in range(1, tiles):
        total = total + load(tile)
    mean = jnp.sum(total, axis=-1, keepdims=True) * (1.0 / width)
    square = jnp.zeros_like(total)
    for tile in range(tiles):
        centred = load(tile) - mean
        square = square + centred * centred
    var = jnp.sum(square, axis=-1, keepdims=True) * (1.0 / width)
    return mean, lax.rsqrt(var + norm_eps)


def front_kernel(
    lens, tok, cot, lnp, turn, freq, wq, bq, wo, wu, bu, wd, bb,
    a_o, b_o, e_o, g_o, du_o, dp_o, o_o, s_o, rows_o, vec_o,
    tok_v, a_v, b_v, e_v, wq_v, wo_v, wu_v, wd_v, st, qkv_v, dkv, o_v, do_v, tabs, mean_v, rstd_v,
    g_v, du_v, buf_wide, buf_cut, buf_x, buf_far, stage, x_own,
    in_sems, st_sems, out_sems, sems,
):
    here = Place()
    rows_all, width = tok_v.shape
    hidden = wu_v.shape[1]
    blocks = rows_all // BLK
    scale = 1.0 / math.sqrt(HS)

    def block_of(i):
        return pl.ds(i * BLK, BLK)

    tok_in = [pltpu.make_async_copy(tok.at[block_of(i)], tok_v.at[block_of(i)], in_sems.at[i]) for i in range(blocks)]
    cot_in = [pltpu.make_async_copy(cot.at[block_of(i)], e_v.at[block_of(i)], in_sems.at[blocks + i]) for i in range(blocks)]
    own_first = here.y * BLK + here.x_hi * HALF
    own_rows = aligned(own_first, HALF)
    x_in = pltpu.make_async_copy(tok.at[own_rows], x_own, in_sems.at[2 * blocks])
    q_in = [pltpu.make_async_copy(wq.at[j], st.at[j], st_sems.at[j]) for j in range(3)]
    wo_in = [
        pltpu.make_async_copy(wo.at[:, pl.ds(k * HS, HS)], st.at[0, pl.ds(k * HS, HS)], st_sems.at[3 + k])
        for k in range(width // HS)
    ]
    up_slot = (1, 2, 0, 1)
    wu_in = [
        pltpu.make_async_copy(wu.at[:, pl.ds(k * HS, HS)], st.at[up_slot[k]], st_sems.at[11 + k])
        for k in range(hidden // HS)
    ]
    down_slot = (2, 2, 0, 0, 1, 1, 2, 2)
    wd_in = [
        pltpu.make_async_copy(
            wd.at[:, pl.ds(k * HS, HS)], st.at[down_slot[k], pl.ds((k % 2) * hidden, hidden)], st_sems.at[15 + k]
        )
        for k in range(width // HS)
    ]
    tok_in[0].start()
    for copy in q_in:
        copy.start()
    for copy in tok_in[1:] + cot_in + [x_in]:
        copy.start()

    end = []
    for j in range(4):
        end.append(lens[0, j] + (end[-1] if j else 0))

    def first_of(t):
        low = jnp.zeros_like(t)
        for j in range(4):
            low = jnp.where(t >= end[j], end[j], low)
        return low

    starts = [jnp.int32(0)] + end[:3]
    lane_row = lax.broadcasted_iota(jnp.int32, (8, 128), 0)
    shift = jnp.zeros((8, 128), jnp.int32)
    for j in range(4):
        shift = jnp.where(lane_row == j, starts[j], shift)
    phase = shift.astype(f32) * freq[...]
    shift_cos, shift_sin = jnp.cos(phase), jnp.sin(phase)

    @pl.loop(0, rows_all // HALF)
    def _(i):
        rows = aligned(i * HALF, HALF)
        t = lax.broadcasted_iota(jnp.int32, (HALF, 128), 0) + i * HALF
        lane = lax.broadcasted_iota(jnp.int32, (HALF, 128), 1)
        c_of = jnp.broadcast_to(shift_cos[0:1], (HALF, 128))
        s_of = jnp.broadcast_to(shift_sin[0:1], (HALF, 128))
        for j in range(1, 4):
            c_of = jnp.where(t >= end[j - 1], shift_cos[j : j + 1], c_of)
            s_of = jnp.where(t >= end[j - 1], shift_sin[j : j + 1], s_of)
        c_of = jnp.where(t >= end[3], shift_cos[4:5], c_of)
        s_of = jnp.where(t >= end[3], shift_sin[4:5], s_of)
        t_cos, t_sin = turn[0, rows], turn[1, rows]
        cos_of = t_cos * c_of + t_sin * s_of
        sin_of = t_sin * c_of - t_cos * s_of
        tabs[0, rows] = cos_of
        tabs[1, rows] = jnp.where(lane < ROT // 2, -sin_of, 0.0)
        tabs[2, rows] = jnp.where((lane >= ROT // 2) & (lane < ROT), sin_of, 0.0)

    chunk = 64

    @pl.loop(0, blocks)
    def _(i):
        pltpu.make_async_copy(tok.at[aligned(i * BLK, BLK)], tok_v.at[aligned(i * BLK, BLK)], in_sems.at[i]).wait()

        @pl.loop(0, BLK // chunk)
        def _(c):
            rows = aligned(i * BLK + c * chunk, chunk)

            def load(tile):
                return tok_v[rows, pl.ds(tile * 128, 128)].astype(f32)

            mean, rstd = row_stats(load, width)
            mean_v[rows] = mean
            rstd_v[rows] = rstd
            for tile in range(width // 128):
                cols = pl.ds(tile * 128, 128)
                normed = (load(tile) - mean) * rstd
                a_v[rows, cols] = (normed * lnp[0:1, cols] + lnp[1:2, cols]).astype(bf16)
                b_v[rows, cols] = (normed * lnp[2:3, cols] + lnp[3:4, cols]).astype(bf16)

    a_out = pltpu.make_async_copy(a_v, a_o, out_sems.at[0])
    b_out = pltpu.make_async_copy(b_v, b_o, out_sems.at[1])
    a_out.start()
    b_out.start()

    def cast(dst, cols, slot, rows_from, rows_count, step=256):
        @pl.loop(0, rows_count // step)
        def _(i):
            dst[aligned(i * step, step), cols] = st[slot, aligned(rows_from + i * step, step), :].astype(bf16)

    for j in range(3):
        q_in[j].wait()
        cast(wq_v, pl.ds(j * HS, HS), j, 0, width)
        if j == 0:
            for copy in wo_in:
                copy.start()
        else:
            wu_in[j - 1].start()

    def turned(wide, sign, rows):
        low = wide[:, :128]
        low = low * tabs[0, rows] + sign * (
            pltpu.roll(low, 128 - ROT // 2, 1) * tabs[1, rows] + pltpu.roll(low, ROT // 2, 1) * tabs[2, rows]
        )
        return jnp.concatenate([low, wide[:, 128:]], axis=1)

    @pl.loop(0, 2)
    def _(j):
        cols = aligned(j * HS, HS)
        out = dot_nn(a_v[...], wq_v[:, cols]) + bq[:, cols]
        qkv_v[:, cols] = turned(out, 1.0, slice(None)).astype(bf16)

    qkv_v[:, 2 * HS :] = (dot_nn(a_v[...], wq_v[:, 2 * HS :]) + bq[:, 2 * HS :]).astype(bf16)

    for copy in wo_in:
        copy.wait()
    for k in range(width // HS):
        cols = pl.ds(k * HS, HS)
        wo_v[:, cols] = st[0, cols, :].astype(bf16)
    wu_in[2].start()
    esum = jnp.zeros((1, width), f32)
    for i in range(blocks):
        cot_in[i].wait()
    vec_o[...] = jnp.zeros_like(vec_o)

    @pl.loop(0, blocks)
    def _(i):
        rows = aligned(i * BLK, BLK)
        t = lax.broadcasted_iota(jnp.int32, (BLK, 1), 0) + i * BLK
        used = (t < end[3]).astype(f32)
        for tile in range(width // 512):
            cols = pl.ds(tile * 512, 512)
            kept = e_v[rows, cols].astype(f32) * used
            e_v[rows, cols] = kept.astype(bf16)
            vec_o[4:5, cols] += jnp.sum(kept, axis=0, keepdims=True)

    e_out = pltpu.make_async_copy(e_v, e_o, out_sems.at[2])
    e_out.start()
    do_v[...] = dot_nt(e_v[...], wo_v[...]).astype(bf16)

    for i in reversed(range(blocks)):
        rows, seen = pl.ds(i * BLK, BLK), (i + 1) * BLK
        query, keys, values = qkv_v[rows, :HS], qkv_v[:seen, HS : 2 * HS], qkv_v[:seen, 2 * HS :]
        t = lax.broadcasted_iota(jnp.int32, (BLK, 1), 0) + i * BLK
        key_at = lax.broadcasted_iota(jnp.int32, (BLK, seen), 1)
        scores = dot_nt(query, keys) * scale
        scores = jnp.where((key_at >= first_of(t)) & (key_at <= t), scores, masked_value)
        weights = jnp.exp(scores - jnp.max(scores, axis=-1, keepdims=True))
        probs = weights * (1.0 / jnp.sum(weights, axis=-1, keepdims=True))
        probs_low = probs.astype(bf16)
        o_v[rows, :] = dot_nn(probs_low, values).astype(bf16)
        grad_mixed = do_v[rows, :]
        grad_probs = dot_nt(grad_mixed, values)
        row_dot = jnp.sum(probs * grad_probs, axis=-1, keepdims=True)
        grad_scores = (probs * (grad_probs - row_dot)).astype(bf16)
        grad_query = dot_nn(grad_scores, keys) * scale
        grad_keys = dot_tn(grad_scores, query) * scale
        grad_values = dot_tn(probs_low, grad_mixed)
        if i == blocks - 1:
            dkv[0] = grad_keys
            dkv[1] = grad_values
        else:
            dkv[0, :seen] += grad_keys
            dkv[1, :seen] += grad_values
        qkv_v[rows, :HS] = turned(grad_query, -1.0, rows).astype(bf16)
    for i in range(blocks):
        rows = pl.ds(i * BLK, BLK)
        qkv_v[rows, HS : 2 * HS] = turned(dkv[0, rows], -1.0, rows).astype(bf16)
        qkv_v[rows, 2 * HS :] = dkv[1, rows].astype(bf16)
    for i in range(blocks):
        vec_o[5:6, : 3 * HS] += jnp.sum(qkv_v[pl.ds(i * BLK, BLK), :].astype(f32), axis=0, keepdims=True)
    o_out = pltpu.make_async_copy(o_v, o_o, out_sems.at[3])
    dp_out = pltpu.make_async_copy(qkv_v, dp_o, out_sems.at[4])
    o_out.start()
    dp_out.start()

    wu_in[0].wait()
    cast(wu_v, pl.ds(0, HS), 1, 0, width)
    wu_in[3].start()
    wu_in[1].wait()
    cast(wu_v, pl.ds(HS, HS), 2, 0, width)
    wd_in[0].start()
    wd_in[1].start()
    wu_in[2].wait()
    cast(wu_v, pl.ds(2 * HS, HS), 0, 0, width)
    wd_in[2].start()
    wd_in[3].start()
    wu_in[3].wait()
    cast(wu_v, pl.ds(3 * HS, HS), 1, 0, width)
    wd_in[4].start()
    wd_in[5].start()
    for k in range(width // HS):
        wd_in[k].wait()
        cast(wd_v, pl.ds(k * HS, HS), down_slot[k], (k % 2) * hidden, hidden)
        if k == 1:
            wd_in[6].start()
            wd_in[7].start()

    a_out.wait()
    z_v = a_v
    greet([here.to_y(here.y_at(1)), here.to_y(here.y_at(3)), here.to_x_hi()])
    branch = BucketSum(here, z_v, buf_wide, buf_cut, buf_x, buf_far, stage, sems, width)

    def feed(off):
        rows = aligned(here.y_at(off) * BLK, BLK)
        up_pre = dot_nn(b_v[rows, :], wu_v[...]) + bu[...]
        grad_act = dot_nt(e_v[rows, :], wd_v[...])
        act, slope = gelu_parts(up_pre)
        g_v[rows, :] = act.astype(bf16)
        grad_low = (grad_act * slope).astype(bf16)
        du_v[rows, :] = grad_low
        vec_o[6:7, :hidden] += jnp.sum(grad_low.astype(f32), axis=0, keepdims=True)

        @pl.loop(0, 2)
        def _(c):
            cols = aligned(c * (width // 2), width // 2)
            z_v[rows, cols] = (dot_nn(o_v[rows, :], wo_v[:, cols]) + dot_nn(g_v[rows, :], wd_v[:, cols])).astype(bf16)

        branch.across[off].start()

    def into_norms(off):
        rows = aligned(here.y_at(off) * BLK, BLK)
        mean, rstd = mean_v[rows], rstd_v[rows]

        @pl.loop(0, 4)
        def _(c):
            cols = aligned(c * (width // 4), width // 4)
            da = dot_nt(qkv_v[rows, :], wq_v[cols, :])
            db = dot_nt(du_v[rows, :], wu_v[cols, :])
            normed = (tok_v[rows, cols].astype(f32) - mean) * rstd
            vec_o[0:1, cols] += jnp.sum(da * normed, axis=0, keepdims=True)
            vec_o[1:2, cols] += jnp.sum(da, axis=0, keepdims=True)
            vec_o[2:3, cols] += jnp.sum(db * normed, axis=0, keepdims=True)
            vec_o[3:4, cols] += jnp.sum(db, axis=0, keepdims=True)
            tok_v[rows, cols] = (da * lnp[0:1, cols] + db * lnp[2:3, cols]).astype(bf16)

    feed(2)
    branch.far.send_opp()
    feed(1)
    branch.far.send_right()
    feed(3)
    branch.far.send_left()
    branch.add_across(2)
    branch.near.send_opp()
    branch.far.relay()
    feed(0)
    g_out = pltpu.make_async_copy(g_v, g_o, out_sems.at[5])
    du_out = pltpu.make_async_copy(du_v, du_o, out_sems.at[6])
    g_out.start()
    du_out.start()
    branch.add_across(1)
    branch.near.send_right()
    branch.add_across(3)
    branch.near.send_left()
    into_norms(2)
    branch.pass_far()
    branch.near.relay()
    into_norms(1)
    branch.add_across(0)
    into_norms(3)
    into_norms(0)
    s_out = pltpu.make_async_copy(tok_v, s_o, out_sems.at[7])
    s_out.start()
    x_in.wait()
    branch.last.got()
    t = lax.broadcasted_iota(jnp.int32, (SUB, 1), 0) + own_first
    for half in range(2):
        rows = pl.ds(half * SUB, SUB)
        total = branch.near.total(half)
        total = jnp.concatenate(
            [total[:, :LEFT_COLS] + buf_far[rows, :].astype(f32), total[:, LEFT_COLS:]], axis=1
        )
        used = (t + half * SUB < end[3]).astype(f32)
        rows_o[rows, :] = (used * (x_own[rows, :].astype(f32) + total + bb[...])).astype(bf16)
    branch.finish()
    for copy in (b_out, e_out, o_out, dp_out, g_out, du_out, s_out):
        copy.wait()


def any_space():
    return pl.BlockSpec(memory_space=pl.ANY)


def vmem_space():
    return pl.BlockSpec(memory_space=pltpu.VMEM)


def rotary_tables(rows):
    inverse = np.exp(np.arange(ROT // 2) * (-2.0 * math.log(10000.0) / ROT))
    angle = np.arange(rows)[:, None] * inverse[None, :]
    cos_of, sin_of = np.ones((rows, 128)), np.zeros((rows, 128))
    freq = np.zeros((8, 128))
    for first in (0, ROT // 2):
        part = slice(first, first + ROT // 2)
        cos_of[:, part], sin_of[:, part] = np.cos(angle), np.sin(angle)
        freq[:, part] = inverse
    return np.stack([cos_of, sin_of]).astype(np.float32), freq.astype(np.float32)


def front(lengths, tokens, cotangent, lnp, wq, bq, wo, wu, bu, wd, bb):
    rows, width = tokens.shape
    hidden = wu.shape[1]
    turn, freq = rotary_tables(rows)
    shape = jax.ShapeDtypeStruct
    outs = (
        shape((rows, width), bf16),
        shape((rows, width), bf16),
        shape((rows, width), bf16),
        shape((rows, hidden), bf16),
        shape((rows, hidden), bf16),
        shape((rows, 3 * HS), bf16),
        shape((rows, HS), bf16),
        shape((rows, width), bf16),
        shape((HALF, width), bf16),
        shape((8, width), f32),
    )
    v = pltpu.VMEM
    dma = pltpu.SemaphoreType.DMA
    return pl.pallas_call(
        front_kernel,
        out_shape=outs,
        in_specs=[
            pl.BlockSpec(memory_space=pltpu.SMEM), any_space(), any_space(), vmem_space(), vmem_space(), vmem_space(),
            any_space(), vmem_space(), any_space(), any_space(), vmem_space(), any_space(), vmem_space(),
        ],
        out_specs=(any_space(),) * 8 + (vmem_space(),) * 2,
        scratch_shapes=[
            v((rows, width), bf16), v((rows, width), bf16), v((rows, width), bf16), v((rows, width), bf16),
            v((width, 3 * HS), bf16), v((HS, width), bf16), v((width, hidden), bf16), v((hidden, width), bf16),
            v((3, width, HS), f32), v((rows, 3 * HS), bf16), v((2, rows, HS), f32), v((rows, HS), bf16),
            v((rows, HS), bf16), v((3, rows, 128), f32), v((rows, 1), f32), v((rows, 1), f32),
            v((rows, hidden), bf16), v((rows, hidden), bf16),
            v((6, SUB, width), bf16), v((6, SUB, LEFT_COLS), bf16), v((4, HALF, width - LEFT_COLS), bf16),
            v((HALF, LEFT_COLS), bf16), v((HALF, LEFT_COLS), bf16), v((HALF, width), bf16),
            dma((9,)), dma((23,)), dma((8,)), dma((2, BucketSum.LINKS)),
        ],
        compiler_params=pltpu.CompilerParams(
            collective_id=0, has_side_effects=True, vmem_limit_bytes=62 * MIB
        ),
        name="front",
    )(lengths, tokens, cotangent, lnp, turn, freq, wq, bq, wo, wu, bu, wd, bb)


class RingCopy:
    def __init__(self, here, own, out, first, cols, sems, base):
        self.out, self.first, self.cols = out, first, cols
        own_y, right, _, left, to_right, to_left = here.ring_y()
        part = self.part
        self.links = [
            Link(sems, base + 0, own, part(own_y), to_right),
            Link(sems, base + 1, own, part(own_y), to_left),
            Link(sems, base + 2, part(left, 0), part(left, 0), to_right),
            Link(sems, base + 3, part(right, 1), part(right, 1), to_left),
        ]

    def part(self, y, half=None, cols=None):
        if half is None:
            rows = aligned(self.first(y), HALF)
        else:
            rows = aligned(self.first(y) + half * SUB, SUB)
        return self.out.at[rows, self.cols if cols is None else cols]

    def start(self):
        self.links[0].start()
        self.links[1].start()

    def pass_on(self):
        for near, far in ((0, 2), (1, 3)):
            self.links[near].got()
            self.links[far].start()

    def finish(self):
        for link in self.links:
            link.sent()


class BucketCopy:
    LINKS = 14

    def __init__(self, here, own, out, sems, local_sem, width):
        cut, rest = pl.ds(0, LEFT_COLS), pl.ds(LEFT_COLS, width - LEFT_COLS)
        first_own = lambda y: y * BLK + here.x_hi * HALF
        first_far = lambda y: y * BLK + (1 - here.x_hi) * HALF
        self.near = RingCopy(here, own, out, first_own, pl.ds(0, width), sems, 0)
        far_own = out.at[aligned(first_far(here.y), HALF), cut]
        self.far = RingCopy(here, far_own, out, first_far, cut, sems, 4)
        part = self.near.part
        y, right, opp, left, _, _ = here.ring_y()
        moves = [(own.at[:, cut], part(y, cols=cut)), (own.at[:, rest], part(y, cols=rest))]
        for place, half in ((left, None), (right, None), (opp, 0), (opp, 1)):
            moves.append((part(place, half, rest), part(place, half, rest)))
        self.across = [Link(sems, 8 + i, src, dst, here.to_x_hi()) for i, (src, dst) in enumerate(moves)]
        self.keep = pltpu.make_async_copy(own, part(y), local_sem)

    def start(self):
        self.near.start()
        self.across[0].start()
        self.across[1].start()
        self.keep.start()

    def start_far(self):
        self.across[0].got()
        self.far.start()

    def pass_near(self):
        self.near.pass_on()
        self.across[2].start()
        self.across[3].start()

    def cross_opp(self):
        for i in range(2):
            self.near.links[2 + i].got()
            self.across[4 + i].start()

    def pass_far(self):
        self.far.pass_on()

    def finish(self):
        self.far.links[2].got()
        self.far.links[3].got()
        for link in self.across[1:]:
            link.got()
        for link in self.across:
            link.sent()
        self.near.finish()
        self.far.finish()
        self.keep.wait()


class GradSum:
    LINKS = 15

    def __init__(self, here, grads, buf_core, buf_ring, stage, buf_last, sems):
        self.here, self.grads, self.buf_core = here, grads, buf_core
        self.stage, self.buf_last = stage, buf_last
        every = pl.ds(0, grads.shape[1])

        def rows(x_lo, z, core):
            return aligned(((x_lo * 4 + z) * 2 + core) * HALF, HALF)

        self.rows = rows
        self.cores = [
            Link(
                sems,
                off * 2 + x_lo,
                grads.at[rows(x_lo, here.z_at(off), 1 - here.core)],
                buf_core.at[off * 2 + x_lo],
                here.to_core(),
            )
            for off in range(4)
            for x_lo in range(2)
        ]
        self.ring = RingSum(
            here.ring_z(), grads, lambda z, half: rows(half, z, here.core), every, buf_ring, sems, 8
        )
        self.last = Link(sems, 14, stage, buf_last, here.to_x_lo())

    def swap(self, off):
        self.cores[off * 2].start()
        self.cores[off * 2 + 1].start()

    def add_core(self, off):
        for x_lo in range(2):
            self.cores[off * 2 + x_lo].got()
            rows = self.rows(x_lo, self.here.z_at(off), self.here.core)
            self.grads[rows, :] = (
                self.grads[rows, :].astype(f32) + self.buf_core[off * 2 + x_lo].astype(f32)
            ).astype(bf16)

    def cross(self, kept):
        low, high = self.ring.total(0), self.ring.total(1)
        mine = self.here.x_lo == 0
        self.stage[...] = jnp.where(mine, high, low).astype(bf16)
        self.last.start()
        kept[...] = jnp.where(mine, low, high)

    def finish(self):
        for link in self.cores + [self.last]:
            link.sent()
        self.ring.finish()


class Total:
    def __init__(self, here, steps, bufs, sems):
        self.steps, self.bufs, self.at = steps, bufs, 0
        z_pair, y_pair = here.z + 1 - 2 * (here.z % 2), here.y + 1 - 2 * (here.y % 2)
        targets = [
            here.to_core(), here.to_z(z_pair), here.to_z(3 - here.z), here.to_x_lo(),
            here.to_y(y_pair), here.to_y(3 - here.y), here.to_x_hi(),
        ]
        self.links = [Link(sems, i, steps.at[i], bufs.at[i], target) for i, target in enumerate(targets)]

    def start(self):
        self.links[0].start()

    def step(self):
        i = self.at
        self.links[i].got()
        self.steps[i + 1] = self.steps[i] + self.bufs[i]
        self.at = i + 1
        if self.at < len(self.links):
            self.links[self.at].start()

    def finish(self):
        for link in self.links:
            link.sent()


def back_kernel(
    tok, a, b, e, g, du, dp, o, s, rows_in, vec,
    out, gt, up_o, down_o, qkv_o, out_o, gains_o, qkv_bias_o, up_bias_o, bias_o,
    a_v, b_v, e_v, g_v, du_v, dp_v, o_v, s_v, x_own, e_own, grads, buf_core, buf_ring, stage_dp, buf_dp, kept,
    buf_wide, buf_cut, buf_x, buf_far, stage, gt_own, steps, step_bufs,
    in_sems, local_sems, sum_sems, out_sems, gt_sems, dp_sems, vec_sems,
):
    here = Place()
    width = s_v.shape[1]
    hidden = g_v.shape[1]
    own_first = here.y * BLK + here.x_hi * HALF
    own_rows = aligned(own_first, HALF)

    pairs = [(s, s_v), (b, b_v), (du, du_v), (e, e_v), (g, g_v), (a, a_v), (dp, dp_v), (o, o_v)]
    pairs += [(tok.at[own_rows], x_own), (e.at[own_rows], e_own)]
    loads = [pltpu.make_async_copy(src, dst, in_sems.at[i]) for i, (src, dst) in enumerate(pairs)]
    for load in loads:
        load.start()

    ring = here.ring_y()
    ring_z = here.ring_z()
    greet([ring[4], ring[5], here.to_x_hi(), ring_z[4], ring_z[5], here.to_core(), here.to_x_lo()])

    wide = BucketSum(here, s_v, buf_wide, buf_cut, buf_x, buf_far, stage, sum_sems, width)
    gather_out = BucketCopy(here, rows_in, out, out_sems, local_sems.at[0], width)
    gather_gt = BucketCopy(here, gt_own, gt, gt_sems, local_sems.at[1], width)
    weights = GradSum(here, grads, buf_core, buf_ring, stage_dp, buf_dp, dp_sems)
    small = Total(here, steps, step_bufs, vec_sems)

    def weight_grads(off):
        @pl.loop(0, 2)
        def _(x_lo):
            m = aligned((x_lo * 4 + here.z_at(off)) * BLK, BLK)
            grads[m, :hidden] = dot_tn(b_v[:, m], du_v[...]).astype(bf16)
            grads[m, hidden : 2 * hidden] = dot_tn(e_v[:, m], g_v[...]).astype(bf16)
            grads[m, 2 * hidden : 2 * hidden + 3 * HS] = dot_tn(a_v[:, m], dp_v[...]).astype(bf16)
            grads[m, 2 * hidden + 3 * HS :] = dot_tn(e_v[:, m], o_v[...]).astype(bf16)

        weights.swap(off)

    loads[0].wait()
    for off in (2, 1, 3, 0):
        wide.across[off].start()
    wide.far.send_opp()
    wide.far.send_right()
    wide.far.send_left()
    steps[0] = vec[...]
    small.start()
    gather_out.start()
    for load in loads[1:]:
        load.wait()

    weight_grads(2)
    wide.add_across(2)
    wide.near.send_opp()
    wide.far.relay()
    small.step()
    weight_grads(1)
    weights.add_core(2)
    weights.ring.send_opp()
    wide.add_across(1)
    wide.near.send_right()
    wide.add_across(3)
    wide.near.send_left()
    wide.pass_far()
    gather_out.start_far()
    small.step()
    weight_grads(3)
    weights.add_core(1)
    weights.ring.send_right()
    wide.add_across(0)
    wide.near.relay()
    gather_out.pass_near()
    small.step()
    weight_grads(0)
    weights.add_core(3)
    weights.ring.send_left()
    weights.add_core(0)
    small.step()

    wide.last.got()
    for half in range(2):
        rows = pl.ds(half * SUB, SUB)
        total = wide.near.total(half)
        total = jnp.concatenate(
            [total[:, :LEFT_COLS] + buf_far[rows, :].astype(f32), total[:, LEFT_COLS:]], axis=1
        )
        x = x_own[rows, :].astype(f32)
        centred = x - jnp.mean(x, axis=-1, keepdims=True)
        rstd = lax.rsqrt(jnp.mean(centred * centred, axis=-1, keepdims=True) + norm_eps)
        normed = centred * rstd
        grad = rstd * (
            total - jnp.mean(total, axis=-1, keepdims=True) - normed * jnp.mean(total * normed, axis=-1, keepdims=True)
        )
        gt_own[rows, :] = (e_own[rows, :].astype(f32) + grad).astype(bf16)
    gather_gt.start()
    small.step()
    gather_out.cross_opp()
    gather_out.pass_far()
    weights.ring.relay()
    small.step()
    gather_gt.start_far()
    small.step()
    gather_gt.pass_near()
    gather_gt.cross_opp()
    gather_gt.pass_far()
    weights.cross(kept)
    gains_o[...] = steps[7, 0:4, aligned(here.mp * HS, HS)]
    bias_o[...] = steps[4, 4:5, aligned(here.mp * HS, HS)]
    qkv_bias_o[...] = steps[4, 5:6, : 3 * HS]
    up_bias_o[...] = steps[4, 6:7, :hidden]
    weights.last.got()
    up_o[...] = kept[:, :hidden] + buf_dp[:, :hidden].astype(f32)
    down_o[...] = (kept[:, hidden : 2 * hidden] + buf_dp[:, hidden : 2 * hidden].astype(f32)).T
    for j in range(3):
        cols = pl.ds(2 * hidden + j * HS, HS)
        qkv_o[j] = kept[:, cols] + buf_dp[:, cols].astype(f32)
    cols = pl.ds(2 * hidden + 3 * HS, HS)
    out_o[...] = (kept[:, cols] + buf_dp[:, cols].astype(f32)).T
    wide.finish()
    weights.finish()
    small.finish()
    gather_out.finish()
    gather_gt.finish()


def back(tokens, a, b, e, g, du, dp, o, s, rows_in, vec):
    rows, width = tokens.shape
    hidden = g.shape[1]
    all_cols = 2 * hidden + 4 * HS
    shape = jax.ShapeDtypeStruct
    outs = (
        shape((rows, width), bf16),
        shape((rows, width), bf16),
        shape((HALF, hidden), f32),
        shape((hidden, HALF), f32),
        shape((3, HALF, HS), f32),
        shape((HS, HALF), f32),
        shape((4, HS), f32),
        shape((1, 3 * HS), f32),
        shape((1, hidden), f32),
        shape((1, HS), f32),
    )
    v = pltpu.VMEM
    dma = pltpu.SemaphoreType.DMA
    return pl.pallas_call(
        back_kernel,
        out_shape=outs,
        in_specs=[any_space()] * 9 + [vmem_space()] * 2,
        out_specs=(any_space(),) * 2 + (vmem_space(),) * 8,
        scratch_shapes=[
            v((rows, width), bf16), v((rows, width), bf16), v((rows, width), bf16), v((rows, hidden), bf16),
            v((rows, hidden), bf16), v((rows, 3 * HS), bf16), v((rows, HS), bf16), v((rows, width), bf16),
            v((HALF, width), bf16), v((HALF, width), bf16),
            v((width, all_cols), bf16), v((8, HALF, all_cols), bf16), v((6, HALF, all_cols), bf16),
            v((HALF, all_cols), bf16), v((HALF, all_cols), bf16), v((HALF, all_cols), f32),
            v((6, SUB, width), bf16), v((6, SUB, LEFT_COLS), bf16), v((4, HALF, width - LEFT_COLS), bf16),
            v((HALF, LEFT_COLS), bf16), v((HALF, LEFT_COLS), bf16), v((HALF, width), bf16),
            v((8, 8, width), f32), v((7, 8, width), f32),
            dma((10,)), dma((2,)), dma((2, BucketSum.LINKS)), dma((2, BucketCopy.LINKS)),
            dma((2, BucketCopy.LINKS)), dma((2, GradSum.LINKS)), dma((2, 7)),
        ],
        compiler_params=pltpu.CompilerParams(
            collective_id=1, has_side_effects=True, vmem_limit_bytes=62 * MIB
        ),
        name="back",
    )(tokens, a, b, e, g, du, dp, o, s, rows_in, vec)


def local(
    tokens, lengths, ln1_gain, ln1_bias, ln2_gain, ln2_bias, qkv_master, qkv_bias, out_master, up_master, up_bias,
    down_master, branch_bias, cotangent,
):
    lnp = jnp.stack([ln1_gain, ln1_bias, ln2_gain, ln2_bias])
    w_qkv = jnp.transpose(qkv_master, (1, 0, 2))
    a, b, e, g, du, dp, o, s, rows, vec = front(
        lengths, tokens, cotangent, lnp, w_qkv, qkv_bias.reshape(1, -1), out_master, up_master,
        up_bias.reshape(1, -1), down_master, branch_bias.reshape(1, -1),
    )
    output, grad_tokens, up, down, qkv, out, gains, qkv_bias_sum, up_bias_sum, bias_sum = back(
        tokens, a, b, e, g, du, dp, o, s, rows, vec
    )
    return (
        output,
        grad_tokens,
        gains[0],
        gains[1],
        gains[2],
        gains[3],
        jnp.transpose(qkv, (1, 0, 2)),
        qkv_bias_sum.reshape(qkv_bias.shape),
        out,
        up,
        up_bias_sum.reshape(up_bias.shape),
        down,
        bias_sum.reshape(-1),
    )


def solution(mesh):
    placed = (
        P("dp", None),
        P("dp", None),
        P(),
        P(),
        P(),
        P(),
        P(None, None, "mp"),
        P(None, "mp"),
        P("mp", None),
        P(None, "mp"),
        P("mp"),
        P("mp", None),
        P(),
        P("dp", None),
    )
    return jax.shard_map(
        local,
        mesh=mesh,
        in_specs=placed,
        out_specs=(
            P("dp", None),
            P("dp", None),
            P("mp"),
            P("mp"),
            P("mp"),
            P("mp"),
            P("dp", None, "mp"),
            P(None, "mp"),
            P("mp", "dp"),
            P("dp", "mp"),
            P("mp"),
            P("mp", "dp"),
            P("mp"),
        ),
        check_vma=False,
    )
```

time: 664 us -> 195 us (0.29)
  waiting for transfers between devices: 388 us -> 0 us
  Pallas kernels: 0 us -> 177 us
  matrix products: 114 us -> 0 us
  blocking collectives: 99.3 us -> 0 us
  other arithmetic: 29.4 us -> 2.09 us
  between operations: 16.4 us -> 0.7 us
    psum x1 -> x0, waiting for transfers between devices: 305 us -> none  [local(): branch_total = lax.psum(branch_part, 'mp')]
    pallas_call x0 -> x2, Pallas kernels: none -> 177 us  [the longest x1 108 us: back(): pl.pallas_call(back_kernel, out_shape=outs, in_specs=[any_space()] * 9 +...]
    dot_general x24 -> x0, matrix products: 114 us -> none  [the longest x4 33.8 us: product_tn(): lax.dot_general(first_mat, second_mat, (((0,), (0,)), ((), ())), preferre...]
    psum x2 -> x0, blocking collectives: 99.3 us -> none  [the longest x1 55.3 us: local(): lax.psum((qkv_bias_grad, up_bias_grad, gain_share, bias_share), 'dp')]
    reduce_scatter x4 -> x0, waiting for transfers between devices: 83.3 us -> none  [the longest x1 76.1 us: local(): lax.psum_scatter(down_weight_grad, 'dp', scatter_dimension=1, tiled=True)]
    reduce_sum x8 -> x0, other arithmetic: 19.1 us -> none  [the longest x1 13.5 us: local(): bias_total = jnp.sum(grad_rows, axis=0)]
    add x5 -> x0, other arithmetic: 6.96 us -> none  [the longest x1 5.81 us: local(): norm_back(attn_grad_in, ln1_gain, normed, inv_std)]
  transfers between devices with their start and end apart: 5 -> 0, of which waited for: 3 -> 0; matrix products, arithmetic and copies ran while one was open for 7% -> 0% of each run, Pallas kernels for 0% -> 0%
where the time goes in v1:
time: 195 us; the launch traced here: 194 us
  Pallas kernels  177 us (91%)
  local copies, waits for them, and re-layouts  14.4 us (7%)
  other arithmetic  2.09 us (1%)
    pallas_call x1, Pallas kernels, back(): pl.pallas_call(back_kernel, out_shape=outs, in_specs=[any_space()] * 9 +...  108 us
    pallas_call x1, Pallas kernels, front(): pl.pallas_call(front_kernel, out_shape=outs, in_specs=[pl.BlockSpec(memor...  69.4 us
    unnamed x23, local copies, waits for them, and re-layouts  12.4 us

profile of v1, /device:TPU:0, one launch (start us, length us, event | category | flops | bytes accessed | tf_op | source)
XLA Modules:
  0.0 194.4 jit_solution(1751516002109638587)
XLA Ops:
  0.6 1.3 copy.29
  1.9 1.4 pad_maximum_fusion.lnp
  3.3 69.4 %front.1 = (bf16[1024,2048]{1,0:T(8,128)(2,1)}, bf16[1024,2048]{1,0:T(8,128)(2,1)}, bf16[1024,2048]{1,0:T(8,128)(2,1)}, bf16[1024,1024]{1,0:T(8,128)(2,1)}, bf16...) custom-call(s32[1,4]{1,0:T(1,128)} %lens.1, ...), custom_call_target="tpu_custom_call" | custom-call | tf_op jit(solution)/shard_map/front/pallas_call | solution.py:565
  72.7 107.8 %back.1 = (bf16[1024,2048]{1,0:T(8,128)(2,1)}, bf16[1024,2048]{1,0:T(8,128)(2,1)}, f32[128,1024]{1,0:T(8,128)}, f32[1024,128]{1,0:T(8,128)}, f32[3,128,256]{2,1,...) custom-call(bf16[1024,2048]{1,0:T(8,128)(2,1)} %tok.3, ...), custom_call_target="tpu_custom_call" | custom-call | tf_op jit(solution)/shard_map/back/pallas_call | solution.py:900
  180.6 0.7 reduce
  181.3 0.6 reshape.47
  181.9 1.4 fusion
  183.3 0.0 copy-start
  183.3 4.9 %copy.38 = bf16[1024,2048]{1,0:T(8,128)(2,1)} copy(bf16[1024,2048]{1,0:T(8,128)(2,1)} %get-tuple-element.70) | data formatting | bytes 8388608
  188.2 0.0 copy-done
  188.2 0.0 copy-start.3
  188.2 0.0 copy-start.4
  188.2 0.0 copy-start.2
  188.2 0.0 copy-start.5
  188.2 0.0 copy-start.1
  188.3 0.0 copy-start.6
  188.3 2.0 %copy.39 = bf16[1024,2048]{1,0:T(8,128)(2,1)} copy(bf16[1024,2048]{1,0:T(8,128)(2,1)S(1)} %copy-done) | data formatting | bytes 8388608
  190.3 0.0 copy-done.3
  190.3 0.7 copy.40
  191.0 0.0 copy-done.4
  191.0 0.7 copy.41
  191.7 0.0 copy-done.2
  191.7 0.8 copy.42
  192.5 0.0 copy-done.5
  192.5 0.6 copy.43
  193.1 0.0 copy-done.1
  193.1 0.8 copy.44
  193.9 0.0 copy-done.6
  193.9 0.6 copy.45
Async XLA Ops:
  183.3 4.9 %copy-start = (bf16[1024,2048]{1,0:T(8,128)(2,1)S(1)}, bf16[1024,2048]{1,0:T(8,128)(2,1)}, u32[]{:S(2)}) copy-start(bf16[1024,2048]{1,0:T(8,128)(2,1)} %get-tuple-element.71) | copy-start | bytes 12582916
  188.2 2.1 %copy-start.3 = (f32[3,128,256]{2,1,0:T(8,128)S(1)}, f32[3,128,256]{2,1,0:T(8,128)}, u32[]{:S(2)}) copy-start(f32[3,128,256]{2,1,0:T(8,128)} %get-tuple-element.46) | copy-start | bytes 1179652
  188.2 2.8 %copy-start.4 = (f32[256,128]{1,0:T(8,128)S(1)}, f32[256,128]{1,0:T(8,128)}, u32[]{:S(2)}) copy-start(f32[256,128]{1,0:T(8,128)} %get-tuple-element.78) | copy-start | bytes 393220
  188.2 3.5 %copy-start.2 = (f32[128,1024]{1,0:T(8,128)S(1)}, f32[128,1024]{1,0:T(8,128)}, u32[]{:S(2)}) copy-start(f32[128,1024]{1,0:T(8,128)} %get-tuple-element.79) | copy-start | bytes 1572868
  188.2 4.3 %copy-start.5 = (f32[1,1024]{1,0:T(1,128)S(1)}, f32[1,1024]{1,0:T(1,128)}, u32[]{:S(2)}) copy-start(f32[1,1024]{1,0:T(1,128)} %get-tuple-element.50) | copy-start | bytes 12292
  188.2 4.8 %copy-start.1 = (f32[1024,128]{1,0:T(8,128)S(1)}, f32[1024,128]{1,0:T(8,128)}, u32[]{:S(2)}) copy-start(f32[1024,128]{1,0:T(8,128)} %get-tuple-element.81) | copy-start | bytes 1572868
  188.3 5.6 %copy-start.6 = (f32[1,256]{1,0:T(1,128)S(1)}, f32[1,256]{1,0:T(1,128)}, u32[]{:S(2)}) copy-start(f32[1,256]{1,0:T(1,128)} %get-tuple-element.52) | copy-start | bytes 3076
